TPU v7x, 128 devices: a whole 4x4x4 slice. The times are simulated.
128 devices in a mesh: pix: 16 (over z, x_lo, core), img: 8 (over x_hi, y).
Axes of the slice: x: 4 (x_hi: 2, x_lo: 2; x = x_hi * 2 + x_lo), y: 4, z: 4, core: 2. Of those that a mesh axis runs over, the one named last changes fastest.
Arguments:
- images: bfloat16 [16384, 16384], P('img', 'pix'), may hold values from -6 to 6
- signs: int32 [16384], P('pix'), may hold values from -1 to 1, as said below
- kept: int32 [512], replicated, may hold values from 0 to 16383, as said below
- omega: bfloat16 [16384, 256], P('img'), may hold values from -0.0625 to 0.0625
Outputs:
- sketch: float32 [256, 512], P('img', 'pix')
Inputs may be any that keep to these rules, and one draw needn't show every extreme that they name: signs are -1 or +1. `kept`: the indices are distinct.
All inputs are finite; a program needn't handle non-finite values.
Results may differ from a plain program's by a relative error of at most 0.0003.
Values sent between devices are 32-bit elements; how exact they have to be, the bound alone decides.
A program may use at most 64 MiB of HBM per device.

v0:
```python
import jax
import jax.numpy as jnp
from jax import lax
from jax.sharding import PartitionSpec as P

NPIX = 16384


def from_partner(array, axis, apart):
    return lax.ppermute(array, axis, [(i, i ^ 1 << apart) for i in range(lax.axis_size(axis))])


def sylvester(count):
    index_row = lax.iota(jnp.int32, count)
    common = index_row[:, None] & index_row[None, :]
    parity = jnp.zeros((count, count), jnp.int32)
    for shift_bit in range((count - 1).bit_length()):
        parity = parity ^ common >> shift_bit & 1
    return 1 - 2 * parity


def compress(values):
    return values / jnp.sqrt(1.0 + values * values)


def local(images, signs, kept, omega):
    width = images.shape[1]
    groups = lax.axis_size("pix")
    place = lax.axis_index("pix")
    scale = float(NPIX) ** (-0.5)
    signed = images * signs.astype(jnp.bfloat16)[None, :]
    local_h = sylvester(width).astype(jnp.bfloat16)
    values = jnp.dot(signed, local_h, preferred_element_type=jnp.float32)
    omega_f = omega.astype(jnp.float32).T
    offset = kept - place * width
    inside = ((offset >= 0) & (offset < width)).astype(jnp.float32)
    column = jnp.clip(offset, 0, width - 1)
    for bit in range(groups.bit_length() - 1):
        partner = from_partner(values, "pix", bit)
        upper = place // (1 << bit) % 2 == 1
        values = jnp.where(upper, partner - values, values + partner)
    picked = jnp.take(values, column, axis=1) * (inside * scale)[None, :]
    partial_sk = jnp.dot(omega_f, compress(picked), precision=lax.Precision.HIGHEST)
    owned = lax.psum_scatter(partial_sk, "pix", scatter_dimension=1, tiled=True)
    return lax.psum_scatter(owned, "img", scatter_dimension=0, tiled=True)


def solution(mesh):
    in_specs = (P("img", "pix"), P("pix"), P(), P("img", None))
    out_specs = P("img", "pix")
    return jax.shard_map(local, mesh=mesh, in_specs=in_specs, out_specs=out_specs, check_vma=False)
```

profile of v0, /device:TPU:0, one launch (start us, length us, event | category | flops | bytes accessed | tf_op | source)
XLA Modules:
  0.0 793.6 jit_solution(16181857077022938648)
XLA Ops:
  6.5 0.8 convert_element_type.8
  7.3 11.6 %fusion.5 = f32[2048,1024]{1,0:T(8,128)} fusion(bf16[2048,1024]{1,0:T(8,128)(2,1)} %param.4, bf16[1024]{0:T(1024)(128)(2,1)S(1)} %convert_element_type.8), kind=kOutput, calls=%fused_computation.13 | convolution fusion | flops 4331667456 | bytes 12584960 | tf_op jit(solution)/shard_map/dot_general | solution.py:33
  19.0 0.0 collective-permute-start
  19.0 13.5 %collective-permute-done = f32[2048,1024]{1,0:T(8,128)} collective-permute-done((f32[2048,1024]{1,0:T(8,128)}, f32[2048,1024]{1,0:T(8,128)}, u32[]{:S(2)}, u32[]{:S(2)}) %collective-permute-start) | collective-permute-done | bytes 8388640 | tf_op jit(solution)/shard_map/ppermute | solution.py:10
  32.5 12.1 %add_select_fusion.3 = f32[2048,1024]{1,0:T(8,128)} fusion(f32[2048,1024]{1,0:T(8,128)} %fusion.5, f32[2048,1024]{1,0:T(8,128)} %collective-permute-done, pred[]{:T(512)S(6)} %eq.20), kind=kLoop, calls=%fused_computation.4 | loop fusion | flops 6291456 | bytes 25165824 | tf_op jit(solution)/shard_map/jit(_where)/select_n | solution.py:41
  44.5 1.6 collective-permute-start.1
  46.1 181.2 %collective-permute-done.1 = f32[2048,1024]{1,0:T(8,128)} collective-permute-done((f32[2048,1024]{1,0:T(8,128)}, f32[2048,1024]{1,0:T(8,128)}, u32[]{:S(2)}, u32[]{:S(2)}) %collective-permute-start.1) | collective-permute-done | bytes 8388640 | tf_op jit(solution)/shard_map/ppermute | solution.py:10
  227.3 12.1 %add_select_fusion.2 = f32[2048,1024]{1,0:T(8,128)} fusion(f32[2048,1024]{1,0:T(8,128)} %add_select_fusion.3, f32[2048,1024]{1,0:T(8,128)} %collective-permute-done.1, pred[]{:T(512)S(6)} %eq.19), kind=kLoop, calls=%fused_computation.3 | loop fusion | flops 6291456 | bytes 25165824 | tf_op jit(solution)/shard_map/jit(_where)/select_n | solution.py:41
  239.4 2.0 collective-permute-start.2
  241.4 180.2 %collective-permute-done.2 = f32[2048,1024]{1,0:T(8,128)} collective-permute-done((f32[2048,1024]{1,0:T(8,128)}, f32[2048,1024]{1,0:T(8,128)}, u32[]{:S(2)}, u32[]{:S(2)}) %collective-permute-start.2) | collective-permute-done | bytes 8388640 | tf_op jit(solution)/shard_map/ppermute | solution.py:10
  421.6 12.1 %add_select_fusion.1 = f32[2048,1024]{1,0:T(8,128)} fusion(f32[2048,1024]{1,0:T(8,128)} %add_select_fusion.2, f32[2048,1024]{1,0:T(8,128)} %collective-permute-done.2, pred[]{:T(512)S(6)} %eq.18), kind=kLoop, calls=%fused_computation.2 | loop fusion | flops 6291456 | bytes 25165824 | tf_op jit(solution)/shard_map/jit(_where)/select_n | solution.py:41
  433.7 3.7 collective-permute-start.3
  437.4 0.0 copy-done.1
  437.5 179.3 %collective-permute-done.3 = f32[2048,1024]{1,0:T(8,128)} collective-permute-done((f32[2048,1024]{1,0:T(8,128)}, f32[2048,1024]{1,0:T(8,128)}, u32[]{:S(2)}, u32[]{:S(2)}) %collective-permute-start.3) | collective-permute-done | bytes 8388640 | tf_op jit(solution)/shard_map/ppermute | solution.py:10
  616.7 12.1 %add_select_fusion = f32[2048,1024]{1,0:T(8,128)} fusion(f32[2048,1024]{1,0:T(8,128)} %add_select_fusion.1, f32[2048,1024]{1,0:T(8,128)} %collective-permute-done.3, pred[]{:T(512)S(6)} %eq.17), kind=kLoop, calls=%fused_computation.1 | loop fusion | flops 6291456 | bytes 25165824 | tf_op jit(solution)/shard_map/jit(_where)/select_n | solution.py:41
  628.8 9.2 %copy.7 = f32[2048,1024]{0,1:T(8,128)} copy(f32[2048,1024]{1,0:T(8,128)} %add_select_fusion) | data formatting | bytes 16777216 | tf_op jit(solution)/shard_map/jit(_where)/select_n | solution.py:41
  638.0 8.8 %gather_fusion = f32[512,2048]{1,0:T(8,128)} fusion(f32[2048,1024]{0,1:T(8,128)} %copy.7, s32[1024]{0:T(1024)S(1)} %pad_clamp_fusion), kind=kCustom, calls=%fused_computation | custom fusion | bytes 8390656 | tf_op jit(solution)/shard_map/jit(_take)/gather | solution.py:42
  646.7 5.8 fusion.22
  652.5 0.0 reduce-scatter.5.cloned.1.call-update
  652.6 0.0 reduce-scatter.7.cloned.1.call-start
  652.6 62.6 %reduce-scatter.5.cloned.1.call-done = f32[256,32]{0,1:T(8,128)} async-done(((f32[256,512]{0,1:T(8,128)}), f32[256,32]{0,1:T(8,128)}) %reduce-scatter.5.cloned.1.call-update) | async-done | bytes 32784 | tf_op jit(solution)/shard_map/reduce_scatter | solution.py:44
  715.3 1.5 copy.9
  716.8 0.0 reduce-scatter.7.cloned.1.call-update
  716.8 70.0 %reduce-scatter.7.cloned.1.call-done = f32[32,32]{1,0:T(8,128)} async-done(((f32[256,32]{1,0:T(8,128)}), f32[32,32]{1,0:T(8,128)}) %reduce-scatter.7.cloned.1.call-update) | async-done | bytes 4112 | tf_op jit(solution)/shard_map/reduce_scatter | solution.py:45
  (7 shorter events, 0.0 us)
Async XLA Ops:
  6.5 640.2 %copy-start = (bf16[2048,256]{1,0:T(8,128)(2,1)S(1)}, bf16[2048,256]{1,0:T(8,128)(2,1)}, u32[]{:S(2)}) copy-start(bf16[2048,256]{1,0:T(8,128)(2,1)} %param.7) | copy-start | bytes 3145732
  6.5 708.7 %reduce-scatter.5.cloned.1.call-start = ((), (), s32[]{:S(2)}) async-start(), calls=%async_computation.2 | async-start | bytes 557056 | tf_op jit(solution)/shard_map/reduce_scatter | solution.py:44
  19.0 13.5 %collective-permute-start = (f32[2048,1024]{1,0:T(8,128)}, f32[2048,1024]{1,0:T(8,128)}, u32[]{:S(2)}, u32[]{:S(2)}) collective-permute-start(f32[2048,1024]{1,0:T(8,128)} %fusion.5), channel_id=1, source_target_pairs={{0,8},{8,0},{16,24},{24,16},{32,40},{40,32},{48,56},{56,48},{64,72... | collective-permute-start | bytes 25165832 | tf_op jit(solution)/shard_map/ppermute | solution.py:10
  44.5 182.8 %collective-permute-start.1 = (f32[2048,1024]{1,0:T(8,128)}, f32[2048,1024]{1,0:T(8,128)}, u32[]{:S(2)}, u32[]{:S(2)}) collective-permute-start(f32[2048,1024]{1,0:T(8,128)} %add_select_fusion.3), channel_id=1, source_target_pairs={{0,16},{8,24},{16,0},{24,8},{32,48},{40,56},{48,32},{56,40},{64,80... | collective-permute-start | bytes 25165832 | tf_op jit(solution)/shard_map/ppermute | solution.py:10
  239.4 182.2 %collective-permute-start.2 = (f32[2048,1024]{1,0:T(8,128)}, f32[2048,1024]{1,0:T(8,128)}, u32[]{:S(2)}, u32[]{:S(2)}) collective-permute-start(f32[2048,1024]{1,0:T(8,128)} %add_select_fusion.2), channel_id=1, source_target_pairs={{0,32},{8,40},{16,48},{24,56},{32,0},{40,8},{48,16},{56,24},{64,96... | collective-permute-start | bytes 25165832 | tf_op jit(solution)/shard_map/ppermute | solution.py:10
  241.4 196.0 %copy-start.1 = (s32[512]{0:T(512)S(1)}, s32[512]{0:T(512)}, u32[]{:S(2)}) copy-start(s32[512]{0:T(512)} %param.6) | copy-start | bytes 6148
  433.7 183.0 %collective-permute-start.3 = (f32[2048,1024]{1,0:T(8,128)}, f32[2048,1024]{1,0:T(8,128)}, u32[]{:S(2)}, u32[]{:S(2)}) collective-permute-start(f32[2048,1024]{1,0:T(8,128)} %add_select_fusion.1), channel_id=1, source_target_pairs={{0,64},{8,72},{16,80},{24,88},{32,96},{40,104},{48,112},{56,120},{... | collective-permute-start | bytes 25165832 | tf_op jit(solution)/shard_map/ppermute | solution.py:10
  652.6 134.2 %reduce-scatter.7.cloned.1.call-start = ((), (), s32[]{:S(2)}) async-start(), calls=%async_computation.3 | async-start | bytes 147456 | tf_op jit(solution)/shard_map/reduce_scatter | solution.py:45
Sparse Core Ops, SparseCore 0:
  652.7 62.5 reduce-scatter.4
  719.2 67.5 reduce-scatter.6
where the time goes:
time: 794 us
  waiting for transfers between devices  687 us (87%)
  other arithmetic  49.1 us (6%)
  local copies, waits for them, and re-layouts  19.5 us (2%)
  matrix products  17.4 us (2%)
  between operations  13.4 us (2%)
    ppermute x4, waiting for transfers between devices, from_partner(): lax.ppermute(array, axis, [(i, i ^ 1 << apart) for i in range(lax.axis_si...  554 us
    reduce_scatter x1, waiting for transfers between devices, local(): return lax.psum_scatter(owned, 'img', scatter_dimension=0, tiled=True)  70 us
    reduce_scatter x1, waiting for transfers between devices, local(): owned = lax.psum_scatter(partial_sk, 'pix', scatter_dimension=1, tiled=True)  62.6 us
    select_n x4, other arithmetic, local(): values = jnp.where(upper, partner - values, values + partner)  48.3 us
  transfers between devices with their start and end apart: 6, of which 6 were waited for; matrix products, arithmetic and copies ran while one was open for 0% of the time, Pallas kernels for 0%

commit v1 on v0

v1 whole, which is shorter than its diff:
```python
import jax
import jax.numpy as jnp
from jax import lax
from jax.sharding import PartitionSpec as P

NPIX = 16384


def hadamard_rows(columns, base, width):
    pixel = base + lax.iota(jnp.int32, width)
    common = columns[:, None] & pixel[None, :]
    return (1 - 2 * (lax.population_count(common) & 1)).astype(jnp.bfloat16)


def local(images, signs, kept, omega):
    width = images.shape[1]
    place = lax.axis_index("pix")
    rows = hadamard_rows(kept, place * width, width) * signs.astype(jnp.bfloat16)[None, :]
    partial = lax.dot_general(rows, images, (((1,), (1,)), ((), ())), preferred_element_type=jnp.float32)
    picked = lax.psum_scatter(partial, "pix", scatter_dimension=0, tiled=True) * float(NPIX) ** (-0.5)
    robust = picked * lax.rsqrt(1.0 + picked * picked)
    sketch = lax.dot_general(
        omega.astype(jnp.float32), robust, (((0,), (1,)), ((), ())), precision=lax.Precision.HIGHEST
    )
    return lax.psum_scatter(sketch, "img", scatter_dimension=0, tiled=True)


def solution(mesh):
    in_specs = (P("img", "pix"), P("pix"), P(), P("img", None))
    out_specs = P("img", "pix")
    return jax.shard_map(local, mesh=mesh, in_specs=in_specs, out_specs=out_specs, check_vma=False)
```

time: 794 us -> 165 us (0.21)
  waiting for transfers between devices: 687 us -> 142 us
  other arithmetic: 49.1 us -> 0.78 us
  local copies, waits for them, and re-layouts: 19.5 us -> 0.74 us
  matrix products: 17.4 us -> 8.2 us
    ppermute x4 -> x0, waiting for transfers between devices: 554 us -> none  [from_partner(): lax.ppermute(array, axis, [(i, i ^ 1 << apart) for i in range(lax.axis_si...]
    select_n x4 -> x0, other arithmetic: 48.3 us -> none  [local(): values = jnp.where(upper, partner - values, values + partner)]
    dot_general x2, matrix products: 17.4 us -> 8.2 us  [the longest x1 6.65 us: local(): lax.dot_general(rows, images, (((1,), (1,)), ((), ())), preferred_element...]
    reduce_scatter x2, waiting for transfers between devices: 133 us -> 142 us  [the longest x1 72.8 us: local(): lax.psum_scatter(partial, 'pix', scatter_dimension=0, tiled=True)]
    select_n x1 -> x0, local copies, waits for them, and re-layouts: 9.15 us -> none  [local(): values = jnp.where(upper, partner - values, values + partner)]
    gather x1 -> x0, local copies, waits for them, and re-layouts: 8.79 us -> none  [local(): picked = jnp.take(values, column, axis=1) * (inside * scale)[None, :]]
  transfers between devices with their start and end apart: 6 -> 2, of which waited for: 6 -> 2; matrix products, arithmetic and copies ran while one was open for 0% -> 0% of each run, Pallas kernels for 0% -> 0%
where the time goes in v1:
time: 165 us
  waiting for transfers between devices  142 us (86%)
  between operations  13.4 us (8%)
  matrix products  8.2 us (5%)
    reduce_scatter x1, waiting for transfers between devices, local(): lax.psum_scatter(partial, 'pix', scatter_dimension=0, tiled=True)  72.8 us
    reduce_scatter x1, waiting for transfers between devices, local(): return lax.psum_scatter(sketch, 'img', scatter_dimension=0, tiled=True)  69 us
    dot_general x1, matrix products, local(): lax.dot_general(rows, images, (((1,), (1,)), ((), ())), preferred_element...  6.65 us
  transfers between devices with their start and end apart: 2, of which 2 were waited for; matrix products, arithmetic and copies ran while one was open for 0% of the time, Pallas kernels for 0%

profile of v1, /device:TPU:0, one launch (start us, length us, event | category | flops | bytes accessed | tf_op | source)
XLA Modules:
  0.0 165.0 jit_solution(11407585414398485780)
XLA Ops:
  6.5 0.0 copy-start
  6.5 0.0 reduce-scatter.5.cloned.1.call-start
  6.5 0.8 convert_element_type.8
  7.3 6.7 %fusion.1 = f32[512,2048]{1,0:T(8,128)} fusion(bf16[2048,1024]{1,0:T(8,128)(2,1)} %param.4, s32[1024]{0:T(1024)S(1)} %iota_add_fusion, s32[512]{0:T(512)} %param.6, bf16[1024]{0:T(1024)(128)(2,1)S(1)} %convert_element_type.8), kind=kOutput, calls=%fused_computation.3 | convolution fusion | flops 2152726528 | bytes 8396800 | tf_op jit(solution)/shard_map/dot_general | solution.py:19
  14.0 0.0 reduce-scatter.5.cloned.1.call-update
  14.0 0.0 reduce-scatter.7.cloned.1.call-start
  14.0 72.8 %reduce-scatter.5.cloned.1.call-done = f32[32,2048]{1,0:T(8,128)} async-done(((f32[512,2048]{1,0:T(8,128)}), f32[32,2048]{1,0:T(8,128)}) %reduce-scatter.5.cloned.1.call-update) | async-done | bytes 262160 | tf_op jit(solution)/shard_map/reduce_scatter | solution.py:20
  86.8 0.0 copy-done
  86.8 1.5 convolution_bitcast_fusion
  88.4 0.7 copy.7
  89.1 0.0 reduce-scatter.7.cloned.1.call-update
  89.2 69.0 %reduce-scatter.7.cloned.1.call-done = f32[32,32]{1,0:T(8,128)} async-done(((f32[256,32]{1,0:T(8,128)}), f32[32,32]{1,0:T(8,128)}) %reduce-scatter.7.cloned.1.call-update) | async-done | bytes 4112 | tf_op jit(solution)/shard_map/reduce_scatter | solution.py:25
  (1 shorter events, 0.0 us)
Async XLA Ops:
  6.5 80.3 %copy-start = (bf16[2048,256]{1,0:T(8,128)(2,1)S(1)}, bf16[2048,256]{1,0:T(8,128)(2,1)}, u32[]{:S(2)}) copy-start(bf16[2048,256]{1,0:T(8,128)(2,1)} %param.7) | copy-start | bytes 3145732
  6.5 80.3 %reduce-scatter.5.cloned.1.call-start = ((), (), s32[]{:S(2)}) async-start(), calls=%async_computation.2 | async-start | bytes 4456448 | tf_op jit(solution)/shard_map/reduce_scatter | solution.py:20
  14.0 144.1 %reduce-scatter.7.cloned.1.call-start = ((), (), s32[]{:S(2)}) async-start(), calls=%async_computation.3 | async-start | bytes 147456 | tf_op jit(solution)/shard_map/reduce_scatter | solution.py:25
Sparse Core Ops, SparseCore 0:
  14.1 72.6 reduce-scatter.4
  90.3 67.7 reduce-scatter.6

commit v2 on v1

v2 whole, which is shorter than its diff:
```python
import functools

import jax
import jax.numpy as jnp
from jax import lax
from jax.experimental import pallas as pl
from jax.experimental.pallas import tpu as pltpu
from jax.sharding import PartitionSpec as P

NPIX = 16384
MESH = pl.DeviceIdType.MESH
KINDS = "BABBABAB"
COUNT = len(KINDS)
LAG = 2
PIECES = ((1, 1), (2, 0), (2, 1), (3, 0), (1, 0), (3, 1), (0, 0), (0, 1))


def transfer(src, dst, send, recv, peer):
    return pltpu.make_async_remote_copy(
        src_ref=src, dst_ref=dst, send_sem=send, recv_sem=recv, device_id=peer, device_id_type=MESH
    )


def kernel(tasks, images, signs_far, kept_far, omega, out, signs, kept, pixels, weights, hada, column, part, fromcore, fromx, z_first, z_second,
           total, slabs, load_sem, send_sem, recv_sem, slab_send, slab_recv):
    place, slab = lax.axis_index("pix"), lax.axis_index("img")
    width = images.shape[1]
    chunk = images.shape[0] // COUNT
    z, x, core = place // 4, place // 2 % 2, place % 2
    sibling = {"pix": z * 4 + x * 2 + (1 - core)}
    across = {"pix": z * 4 + (1 - x) * 2 + core}
    above = {"pix": (z + 1) % 4 * 4 + x * 2 + core}
    below = {"pix": (z + 3) % 4 * 4 + x * 2 + core}
    others = [{"img": (slab + step) % 8} for step in range(1, 8)]

    loads = [
        pltpu.make_async_copy(images.at[pl.ds(i * chunk, chunk)], pixels.at[i], load_sem.at[i]) for i in range(COUNT)
    ]
    loads.append(pltpu.make_async_copy(omega, weights, load_sem.at[COUNT]))
    small = [
        pltpu.make_async_copy(kept_far, kept, load_sem.at[COUNT + 1]),
        pltpu.make_async_copy(signs_far, signs, load_sem.at[COUNT + 2]),
    ]
    for load in small + loads:
        load.start()
    barrier = pltpu.get_barrier_semaphore()
    for peer in [sibling, across, above, below] + others:
        pl.semaphore_signal(barrier, inc=1, device_id=peer, device_id_type=MESH)

    for load in small:
        load.wait()
    for i in range(4):
        row = kept[pl.ds(i * 128, 128)].reshape(1, 128)
        column[i * 128:(i + 1) * 128, :] = jnp.broadcast_to(row, (128, 128)).T
    lane = lax.broadcasted_iota(jnp.int32, (32, 128), 1)
    marks = [signs[pl.ds(j * 128, 128)].reshape(1, 128).astype(jnp.float32) for j in range(width // 128)]

    def sign_of(bits):
        return (1 - 2 * (lax.population_count(bits) & 1)).astype(jnp.float32)

    for rc in range(2):
        for rx in range(2):
            for rz in range(4):
                owner = (z + rz) % 4 * 4 + (x + rx) % 2 * 2 + (core + rc) % 2
                index = column[pl.ds(pl.multiple_of(owner * 32, 32), 32), :]
                low = sign_of(index & (lane + place * width))
                flips = [(1 - 2 * (index >> b & 1)).astype(jnp.float32) for b in (7, 8, 9)]
                halves = [(rc * 2 + rx) * 128 + PIECES.index((rz, half)) * 16 for half in range(2)]
                for j in range(width // 128):
                    value = low * marks[j]
                    for b in range(3):
                        if j >> b & 1:
                            value = value * flips[b]
                    value = value.astype(jnp.bfloat16)
                    for half in range(2):
                        hada[halves[half]:halves[half] + 16, j * 128:(j + 1) * 128] = value[half * 16:half * 16 + 16]

    sends = {}
    used = iter(range(1000))

    def start(key, src, dst, peer):
        at = next(used)
        copy = transfer(src, dst, send_sem.at[at], recv_sem.at[at], peer)
        copy.start()
        sends[key] = copy

    def kinds(i):
        return slice(0, 1) if KINDS[i] == "A" else slice(0, 2)

    def multiply(i, rc):
        value = lax.dot_general(
            hada[rc * 256:(rc + 1) * 256, :], pixels[i], (((1,), (1,)), ((), ())), preferred_element_type=jnp.float32
        )
        part[i, rc] = value.reshape(2, 8, 16, chunk)

    def first_round(i):
        rx = kinds(i)
        start(("up", i), part.at[i, 0, rx, 0:2], z_first.at[i, 0, rx], above)
        start(("down", i), part.at[i, 0, rx, 2:4], z_first.at[i, 1, rx], below)

    def core_done(i):
        sends["core", i].wait_recv()
        part[i, 0] = part[i, 0] + fromcore[i]
        if KINDS[i] == "A":
            start(("x", i), part.at[i, 0, 1], fromx.at[i], across)
        else:
            first_round(i)

    def x_done(i):
        sends["x", i].wait_recv()
        part[i, 0, 0] = part[i, 0, 0] + fromx[i]
        first_round(i)

    def first_done(i):
        rx = kinds(i)
        sends["up", i].wait_recv()
        part[i, 0, rx, 4] = part[i, 0, rx, 4] + z_first[i, 0, rx, 1]
        start(("up2", i), part.at[i, 0, rx, 4], z_second.at[i, 0, rx], above)
        sends["down", i].wait_recv()
        part[i, 0, rx, 5] = part[i, 0, rx, 5] + z_first[i, 1, rx, 0]
        start(("down2", i), part.at[i, 0, rx, 5], z_second.at[i, 1, rx], below)

    def ring_sum(i, rx):
        upper = part[i, 0, rx, 6] + z_first[i, 1, rx, 1] + z_second[i, 0, rx]
        lower = part[i, 0, rx, 7] + z_first[i, 0, rx, 0] + z_second[i, 1, rx]
        return upper, lower

    def second_done(i):
        sends["up2", i].wait_recv()
        sends["down2", i].wait_recv()
        if KINDS[i] == "A":
            finish(i, ring_sum(i, 0))
        else:
            upper, lower = ring_sum(i, 1)
            part[i, 0, 1, 6] = upper
            part[i, 0, 1, 7] = lower
            start(("late", i), part.at[i, 0, 1, 6:8], fromx.at[i, 0:2], across)

    def late_done(i):
        sends["late", i].wait_recv()
        upper, lower = ring_sum(i, 0)
        finish(i, (upper + fromx[i, 0], lower + fromx[i, 1]))

    def finish(i, halves):
        picked = jnp.concatenate(halves, axis=0) * float(NPIX) ** (-0.5)
        robust = picked * lax.rsqrt(1.0 + picked * picked)
        high = robust.astype(jnp.bfloat16)
        rest = (robust - high.astype(jnp.float32)).astype(jnp.bfloat16)
        both = jnp.concatenate([high, rest], axis=0)
        term = jnp.dot(both, weights[pl.ds(i * chunk, chunk), :], preferred_element_type=jnp.float32)
        sketch.append(term[:32] + term[32:])

    sketch = []
    for i in range(COUNT):
        loads[i].wait()
        multiply(i, 1)
        if i == 0:
            pl.semaphore_wait(barrier, 4 + len(others))
        start(("core", i), part.at[i, 1], fromcore.at[i], sibling)
        multiply(i, 0)
        if i >= LAG:
            core_done(i - LAG)
    for i in range(COUNT - LAG, COUNT):
        core_done(i)
    loads[COUNT].wait()
    steps = dict(x=x_done, f=first_done, s=second_done, l=late_done)
    for name, i in tasks:
        steps[name](i)

    whole = functools.reduce(lambda a, b: a + b, sketch)
    total[0] = whole[:, :128]
    total[1] = whole[:, 128:]
    final = []
    for step, peer in enumerate(others):
        copy = transfer(total.at[peer["img"] // 4], slabs.at[step], slab_send.at[step], slab_recv.at[step], peer)
        copy.start()
        final.append(copy)
    for copy in sends.values():
        copy.wait_send()
    result = total[slab // 4]
    for step, copy in enumerate(final):
        copy.wait_recv()
        result = result + slabs[step]
    turned = jnp.concatenate([result, jnp.zeros((96, 128), jnp.float32)], axis=0).T
    column_block = [turned[32 * n:32 * n + 32, 0:32] for n in range(4)]
    mine = column_block[0]
    for n in range(1, 4):
        mine = jnp.where(slab % 4 == n, column_block[n], mine)
    out[...] = mine
    for copy in final:
        copy.wait_send()


def default_tasks():
    tasks = []
    for i in range(COUNT):
        if KINDS[i] == "B":
            tasks.append(("f", i))
        else:
            tasks.append(("x", i))
    for i in range(COUNT):
        if KINDS[i] == "B":
            tasks.append(("s", i))
        else:
            tasks.append(("f", i))
    for i in range(COUNT):
        if KINDS[i] == "B":
            tasks.append(("l", i))
        else:
            tasks.append(("s", i))
    return tasks


def local(images, signs, kept, omega):
    rows, width = images.shape
    chunk = rows // COUNT
    copies = 6 * COUNT
    return pl.pallas_call(
        functools.partial(kernel, default_tasks()),
        out_shape=jax.ShapeDtypeStruct((32, 32), jnp.float32),
        in_specs=[
            pl.BlockSpec(memory_space=pltpu.HBM),
            pl.BlockSpec(memory_space=pltpu.HBM),
            pl.BlockSpec(memory_space=pltpu.HBM),
            pl.BlockSpec(memory_space=pltpu.HBM),
        ],
        out_specs=pl.BlockSpec(memory_space=pltpu.VMEM),
        scratch_shapes=[
            pltpu.VMEM(signs.shape, jnp.int32),
            pltpu.VMEM(kept.shape, jnp.int32),
            pltpu.VMEM((COUNT, chunk, width), jnp.bfloat16),
            pltpu.VMEM(omega.shape, jnp.bfloat16),
            pltpu.VMEM((512, width), jnp.bfloat16),
            pltpu.VMEM((512, 128), jnp.int32),
            pltpu.VMEM((COUNT, 2, 2, 8, 16, chunk), jnp.float32),
            pltpu.VMEM((COUNT, 2, 8, 16, chunk), jnp.float32),
            pltpu.VMEM((COUNT, 8, 16, chunk), jnp.float32),
            pltpu.VMEM((COUNT, 2, 2, 2, 16, chunk), jnp.float32),
            pltpu.VMEM((COUNT, 2, 2, 16, chunk), jnp.float32),
            pltpu.VMEM((2, 32, 128), jnp.float32),
            pltpu.VMEM((7, 32, 128), jnp.float32),
            pltpu.SemaphoreType.DMA((COUNT + 3,)),
            pltpu.SemaphoreType.DMA((copies,)),
            pltpu.SemaphoreType.DMA((copies,)),
            pltpu.SemaphoreType.DMA((7,)),
            pltpu.SemaphoreType.DMA((7,)),
        ],
        compiler_params=pltpu.CompilerParams(collective_id=0, has_side_effects=True, vmem_limit_bytes=64 << 20),
        cost_estimate=pl.CostEstimate(flops=2 * rows * width * 512, bytes_accessed=5 << 20, transcendentals=0),
        name="sketch",
    )(images, signs, kept, omega)


def solution(mesh):
    in_specs = (P("img", "pix"), P("pix"), P(), P("img", None))
    out_specs = P("img", "pix")
    return jax.shard_map(local, mesh=mesh, in_specs=in_specs, out_specs=out_specs, check_vma=False)
```

time: 165 us -> 36.9 us (0.22)
  waiting for transfers between devices: 142 us -> 0 us
  Pallas kernels: 0 us -> 35.4 us
  between operations: 13.4 us -> 0.01 us
  matrix products: 8.2 us -> 0 us
    reduce_scatter x2 -> x0, waiting for transfers between devices: 142 us -> none  [the longest x1 72.8 us: local(): lax.psum_scatter(partial, 'pix', scatter_dimension=0, tiled=True)]
    pallas_call x0 -> x1, Pallas kernels: none -> 35.4 us  [local(): pl.pallas_call(functools.partial(kernel, default_tasks()), out_shape=jax....]
    dot_general x2 -> x0, matrix products: 8.2 us -> none  [the longest x1 6.65 us: local(): lax.dot_general(rows, images, (((1,), (1,)), ((), ())), preferred_element...]
  transfers between devices with their start and end apart: 2 -> 0, of which waited for: 2 -> 0; matrix products, arithmetic and copies ran while one was open for 0% -> 0% of each run, Pallas kernels for 0% -> 0%
where the time goes in v2:
time: 36.9 us; the launch traced here: 36.7 us
  Pallas kernels  35.4 us (96%)
  local copies, waits for them, and re-layouts  1.32 us (4%)
    pallas_call x1, Pallas kernels, local(): pl.pallas_call(functools.partial(kernel, default_tasks()), out_shape=jax....  35.4 us
    unnamed x1, local copies, waits for them, and re-layouts  1.32 us

profile of v2, /device:TPU:0, one launch (start us, length us, event | category | flops | bytes accessed | tf_op | source)
XLA Modules:
  0.0 36.7 jit_solution(12107950376016569756)
XLA Ops:
  0.0 35.4 %sketch.1 = f32[32,32]{1,0:T(8,128)} custom-call(bf16[2048,1024]{1,0:T(8,128)(2,1)} %images.1, s32[1024]{0:T(1024)} %signs_far.1, s32[512]{0:T(512)} %kept_far.1, bf16[2048,256]{1,0:T(8,128)(2,1)} %omega.1), custom_call_target="tpu_custom_call" | custom-call | flops 2147483648 | bytes 5242880 | tf_op jit(solution)/shard_map/sketch/pallas_call | solution.py:218
  35.4 1.3 %copy.6 = f32[32,32]{1,0:T(8,128)} copy(f32[32,32]{1,0:T(8,128)} %sketch.1) | data formatting | bytes 8192

commit v3 on v2

v3 whole, which is shorter than its diff:
```python
import functools

import jax
import jax.numpy as jnp
from jax import lax
from jax.experimental import pallas as pl
from jax.experimental.pallas import tpu as pltpu
from jax.sharding import PartitionSpec as P

NPIX = 16384
MESH = pl.DeviceIdType.MESH
CHUNKS = (
    ("B", 128), ("A", 128), ("B", 256), ("A", 256), ("B", 256), ("A", 256), ("B", 256), ("A", 256), ("B", 256),
)
COUNT = len(CHUNKS)
STARTS = [sum(size for _, size in CHUNKS[:i]) for i in range(COUNT)]
GROUPS = ((0, 2), (2, 2), (4, 2), (6, 3))
ORDER = (
    ("m", 0), ("m", 1), ("c", 0), ("c", 1), ("m", 2), ("c", 2), ("c", 3), ("m", 3), ("c", 4), ("f", 0),
    ("c", 5), ("x", 1), ("c", 6), ("c", 7), ("f", 2), ("c", 8), ("f", 4), ("x", 3), ("s", 0), ("f", 1),
    ("f", 6), ("s", 2), ("x", 5), ("f", 8), ("s", 4), ("x", 7), ("f", 3), ("s", 1), ("l", 0), ("s", 6),
    ("l", 2), ("f", 5), ("l", 4), ("s", 8), ("f", 7), ("s", 3), ("l", 6), ("s", 5), ("l", 8), ("s", 7),
)
PIECES = ((1, 1), (2, 0), (2, 1), (3, 0), (1, 0), (3, 1), (0, 0), (0, 1))


def transfer(src, dst, send, recv, peer):
    return pltpu.make_async_remote_copy(
        src_ref=src, dst_ref=dst, send_sem=send, recv_sem=recv, device_id=peer, device_id_type=MESH
    )


def kernel(images, signs_far, kept_far, omega, out, signs, kept, pixels, weights, hada, column, total, packed, slabs,
           load_sem, send_sem, recv_sem, slab_send, slab_recv, near, far, *buffers):
    part, fromcore, fromx, z_first, z_second = (buffers[n * COUNT:(n + 1) * COUNT] for n in range(5))
    place, slab = lax.axis_index("pix"), lax.axis_index("img")
    width = images.shape[1]
    z, x, core = place // 4, place // 2 % 2, place % 2
    sibling = {"pix": z * 4 + x * 2 + (1 - core)}
    across = {"pix": z * 4 + (1 - x) * 2 + core}
    above = {"pix": (z + 1) % 4 * 4 + x * 2 + core}
    below = {"pix": (z + 3) % 4 * 4 + x * 2 + core}
    others = [{"img": (slab + step) % 8} for step in range(1, 8)]

    loads = []
    for i, (_, size) in enumerate(CHUNKS):
        here = pl.ds(STARTS[i], size)
        loads.append(pltpu.make_async_copy(images.at[here], pixels.at[here], load_sem.at[i]))
    loads.append(pltpu.make_async_copy(omega, weights, load_sem.at[COUNT]))
    small = [
        pltpu.make_async_copy(kept_far, kept, load_sem.at[COUNT + 1]),
        pltpu.make_async_copy(signs_far, signs, load_sem.at[COUNT + 2]),
    ]
    for load in small + loads:
        load.start()
    barrier = pltpu.get_barrier_semaphore()
    beside = [{"img": slab // 4 * 4 + (slab + step) % 4} for step in (1, 3)] + [{"img": (slab + 4) % 8}]
    greeted = [sibling, across, above, below] + beside
    for peer in greeted:
        pl.semaphore_signal(barrier, inc=1, device_id=peer, device_id_type=MESH)

    def tell(known):
        for peer in beside:
            pl.semaphore_signal(known, inc=1, device_id=peer, device_id_type=MESH)

    def hear(known):
        pl.semaphore_wait(known, len(beside))

    for load in small:
        load.wait()
    for i in range(4):
        row = kept[pl.ds(i * 128, 128)].reshape(1, 128)
        column[i * 128:(i + 1) * 128, :] = jnp.broadcast_to(row, (128, 128)).T
    lane = lax.broadcasted_iota(jnp.int32, (32, 128), 1)
    marks = [signs[pl.ds(j * 128, 128)].reshape(1, 128).astype(jnp.float32) for j in range(width // 128)]

    def sign_of(bits):
        return (1 - 2 * (lax.population_count(bits) & 1)).astype(jnp.float32)

    for rc in (1, 0):
        for rx in range(2):
            for rz in range(4):
                owner = (z + rz) % 4 * 4 + (x + rx) % 2 * 2 + (core + rc) % 2
                index = column[pl.ds(pl.multiple_of(owner * 32, 32), 32), :]
                low = sign_of(index & (lane + place * width))
                flips = [(1 - 2 * (index >> b & 1)).astype(jnp.float32) for b in (7, 8, 9)]
                halves = [(rc * 2 + rx) * 128 + PIECES.index((rz, half)) * 16 for half in range(2)]
                for j in range(width // 128):
                    value = low * marks[j]
                    for b in range(3):
                        if j >> b & 1:
                            value = value * flips[b]
                    value = value.astype(jnp.bfloat16)
                    for half in range(2):
                        hada[halves[half]:halves[half] + 16, j * 128:(j + 1) * 128] = value[half * 16:half * 16 + 16]

    sends = {}

    def start(key, src, dst, peer):
        at = len(sends)
        copy = transfer(src, dst, send_sem.at[at], recv_sem.at[at], peer)
        copy.start()
        sends[key] = copy

    def lines(i):
        return slice(0, 1) if CHUNKS[i][0] == "A" else slice(0, 2)

    def matmul(group):
        first, count = GROUPS[group]
        size = sum(CHUNKS[i][1] for i in range(first, first + count))
        for i in range(first, first + count):
            loads[i].wait()
        value = lax.dot_general(
            hada[...], pixels[pl.ds(STARTS[first], size), :], (((1,), (1,)), ((), ())), preferred_element_type=jnp.float32
        )
        for i in range(first, first + count):
            at = STARTS[i] - STARTS[first]
            part[i][...] = value[:, at:at + CHUNKS[i][1]].reshape(part[i].shape)
        if first == 0:
            pl.semaphore_wait(barrier, len(greeted))
        for i in range(first, first + count):
            start(("core", i), part[i].at[1], fromcore[i], sibling)

    def first_round(i):
        rx = lines(i)
        start(("up", i), part[i].at[0, rx, 0:2], z_first[i].at[0], above)
        start(("down", i), part[i].at[0, rx, 2:4], z_first[i].at[1], below)

    def core_done(i):
        sends["core", i].wait_recv()
        if CHUNKS[i][0] == "A":
            part[i][0, 1] = part[i][0, 1] + fromcore[i][1]
            start(("x", i), part[i].at[0, 1], fromx[i], across)
            part[i][0, 0] = part[i][0, 0] + fromcore[i][0]
        else:
            part[i][0, :, 0:4] = part[i][0, :, 0:4] + fromcore[i][:, 0:4]
            first_round(i)
            part[i][0, :, 4:8] = part[i][0, :, 4:8] + fromcore[i][:, 4:8]

    def x_done(i):
        sends["x", i].wait_recv()
        part[i][0, 0, 0:4] = part[i][0, 0, 0:4] + fromx[i][0:4]
        first_round(i)
        part[i][0, 0, 4:8] = part[i][0, 0, 4:8] + fromx[i][4:8]

    def first_done(i):
        rx = lines(i)
        sends["up", i].wait_recv()
        part[i][0, rx, 4] = part[i][0, rx, 4] + z_first[i][0, :, 1]
        start(("up2", i), part[i].at[0, rx, 4], z_second[i].at[0], above)
        sends["down", i].wait_recv()
        part[i][0, rx, 5] = part[i][0, rx, 5] + z_first[i][1, :, 0]
        start(("down2", i), part[i].at[0, rx, 5], z_second[i].at[1], below)

    def ring_sum(i, rx):
        upper = part[i][0, rx, 6] + z_first[i][1, rx, 1] + z_second[i][0, rx]
        lower = part[i][0, rx, 7] + z_first[i][0, rx, 0] + z_second[i][1, rx]
        return upper, lower

    def second_done(i):
        sends["up2", i].wait_recv()
        sends["down2", i].wait_recv()
        if CHUNKS[i][0] == "A":
            finish(i, ring_sum(i, 0))
        else:
            upper, lower = ring_sum(i, 1)
            part[i][0, 1, 6] = upper
            part[i][0, 1, 7] = lower
            start(("late", i), part[i].at[0, 1, 6:8], fromx[i], across)
            upper, lower = ring_sum(i, 0)
            part[i][0, 0, 6] = upper
            part[i][0, 0, 7] = lower

    def late_done(i):
        sends["late", i].wait_recv()
        finish(i, (part[i][0, 0, 6] + fromx[i][0], part[i][0, 0, 7] + fromx[i][1]))

    finished = []

    def finish(i, halves):
        picked = jnp.concatenate(halves, axis=0) * float(NPIX) ** (-0.5)
        robust = picked * lax.rsqrt(1.0 + picked * picked)
        high = robust.astype(jnp.bfloat16)
        rest = (robust - high.astype(jnp.float32)).astype(jnp.bfloat16)
        both = jnp.concatenate([high, rest], axis=0)
        if not finished:
            loads[COUNT].wait()
        term = jnp.dot(both, weights[pl.ds(STARTS[i], CHUNKS[i][1]), :], preferred_element_type=jnp.float32)
        term = term[:32] + term[32:]
        for n in range(2):
            fresh = term[:, n * 128:(n + 1) * 128]
            total[n] = total[n] + fresh if finished else fresh
        finished.append(i)

    steps = dict(m=matmul, c=core_done, x=x_done, f=first_done, s=second_done, l=late_done)
    for at, (name, i) in enumerate(ORDER):
        steps[name](i)
        if at == len(ORDER) // 4:
            tell(near)
        if at == len(ORDER) // 2:
            hear(near)
            tell(far)
    hear(far)

    for n in range(8):
        lanes = slice(n % 4 * 32, n % 4 * 32 + 32)
        packed[n] = jnp.concatenate([total[n // 4, 8 * q:8 * q + 8, lanes] for q in range(4)], axis=1)
    final = []
    for step, peer in enumerate(others):
        copy = transfer(packed.at[peer["img"]], slabs.at[step], slab_send.at[step], slab_recv.at[step], peer)
        copy.start()
        final.append(copy)
    for copy in sends.values():
        copy.wait_send()
    result = packed[slab]
    for step, copy in enumerate(final):
        copy.wait_recv()
        result = result + slabs[step]
    block = jnp.concatenate([result[:, 32 * q:32 * q + 32] for q in range(4)], axis=0)
    out[...] = block.T
    for copy in final:
        copy.wait_send()


def local(images, signs, kept, omega):
    rows, width = images.shape
    copies = 6 * COUNT
    scratch = [
        pltpu.VMEM(signs.shape, jnp.int32),
        pltpu.VMEM(kept.shape, jnp.int32),
        pltpu.VMEM((rows, width), jnp.bfloat16),
        pltpu.VMEM(omega.shape, jnp.bfloat16),
        pltpu.VMEM((512, width), jnp.bfloat16),
        pltpu.VMEM((512, 128), jnp.int32),
        pltpu.VMEM((2, 32, 128), jnp.float32),
        pltpu.VMEM((8, 8, 128), jnp.float32),
        pltpu.VMEM((7, 8, 128), jnp.float32),
        pltpu.SemaphoreType.DMA((COUNT + 3,)),
        pltpu.SemaphoreType.DMA((copies,)),
        pltpu.SemaphoreType.DMA((copies,)),
        pltpu.SemaphoreType.DMA((7,)),
        pltpu.SemaphoreType.DMA((7,)),
        pltpu.SemaphoreType.REGULAR,
        pltpu.SemaphoreType.REGULAR,
    ]
    lines = [1 if kind == "A" else 2 for kind, _ in CHUNKS]
    scratch += [pltpu.VMEM((2, 2, 8, 16, size), jnp.float32) for _, size in CHUNKS]
    scratch += [pltpu.VMEM((2, 8, 16, size), jnp.float32) for _, size in CHUNKS]
    scratch += [pltpu.VMEM((8 if kind == "A" else 2, 16, size), jnp.float32) for kind, size in CHUNKS]
    scratch += [pltpu.VMEM((2, n, 2, 16, size), jnp.float32) for n, (_, size) in zip(lines, CHUNKS)]
    scratch += [pltpu.VMEM((2, n, 16, size), jnp.float32) for n, (_, size) in zip(lines, CHUNKS)]
    return pl.pallas_call(
        kernel,
        out_shape=jax.ShapeDtypeStruct((32, 32), jnp.float32),
        in_specs=[pl.BlockSpec(memory_space=pl.ANY)] * 4,
        out_specs=pl.BlockSpec(memory_space=pltpu.VMEM),
        scratch_shapes=scratch,
        compiler_params=pltpu.CompilerParams(collective_id=0, has_side_effects=True, vmem_limit_bytes=48 << 20),
        cost_estimate=pl.CostEstimate(flops=2 * rows * width * 512, bytes_accessed=5 << 20, transcendentals=0),
        name="sketch",
    )(*(pltpu.with_memory_space_constraint(array, pltpu.HBM) for array in (images, signs, kept, omega)))


def solution(mesh):
    in_specs = (P("img", "pix"), P("pix"), P(), P("img", None))
    out_specs = P("img", "pix")
    return jax.shard_map(local, mesh=mesh, in_specs=in_specs, out_specs=out_specs, check_vma=False)
```

time: 36.9 us -> 33.1 us (0.90)
  Pallas kernels: 35.4 us -> 32.4 us
  local copies, waits for them, and re-layouts: 1.32 us -> 0.61 us
    pallas_call x1, Pallas kernels: 35.4 us -> 32.4 us  [local(): pl.pallas_call(kernel, out_shape=jax.ShapeDtypeStruct((32, 32), jnp.float...]
    unnamed x1, local copies, waits for them, and re-layouts: 1.32 us -> 0.61 us
where the time goes in v3:
time: 33.1 us; the launch traced here: 33 us
  Pallas kernels  32.4 us (98%)
  local copies, waits for them, and re-layouts  0.61 us (2%)
    pallas_call x1, Pallas kernels, local(): pl.pallas_call(kernel, out_shape=jax.ShapeDtypeStruct((32, 32), jnp.float...  32.4 us

profile of v3, /device:TPU:0, one launch (start us, length us, event | category | flops | bytes accessed | tf_op | source)
XLA Modules:
  0.0 33.0 jit_solution(3540452529861874374)
XLA Ops:
  0.0 32.4 %sketch.1 = f32[32,32]{1,0:T(8,128)S(1)} custom-call(bf16[2048,1024]{1,0:T(8,128)(2,1)} %images.1, s32[1024]{0:T(1024)} %signs_far.1, s32[512]{0:T(512)} %kept_far.1, bf16[2048,256]{1,0:T(8,128)(2,1)} %omega.1), custom_call_target="tpu_custom_call" | custom-call | flops 2147483648 | bytes 5242880 | tf_op jit(solution)/shard_map/sketch/pallas_call | solution.py:252
  32.4 0.6 %copy.6 = f32[32,32]{1,0:T(8,128)} copy(f32[32,32]{1,0:T(8,128)S(1)} %sketch.1) | data formatting | bytes 8192

commit v4 on v3

--- a/solution.py
+++ b/solution.py
@@ -10,16 +10,17 @@
 NPIX = 16384
 MESH = pl.DeviceIdType.MESH
 CHUNKS = (
-    ("B", 128), ("A", 128), ("B", 256), ("A", 256), ("B", 256), ("A", 256), ("B", 256), ("A", 256), ("B", 256),
+    ("B", 256), ("B", 256), ("A", 256), ("B", 384), ("A", 128), ("A", 256), ("B", 128), ("B", 256), ("A", 128),
 )
 COUNT = len(CHUNKS)
 STARTS = [sum(size for _, size in CHUNKS[:i]) for i in range(COUNT)]
-GROUPS = ((0, 2), (2, 2), (4, 2), (6, 3))
+GROUPS = ((0, 1), (1, 2), (3, 2), (5, 2), (7, 1), (8, 1))
 ORDER = (
-    ("m", 0), ("m", 1), ("c", 0), ("c", 1), ("m", 2), ("c", 2), ("c", 3), ("m", 3), ("c", 4), ("f", 0),
-    ("c", 5), ("x", 1), ("c", 6), ("c", 7), ("f", 2), ("c", 8), ("f", 4), ("x", 3), ("s", 0), ("f", 1),
-    ("f", 6), ("s", 2), ("x", 5), ("f", 8), ("s", 4), ("x", 7), ("f", 3), ("s", 1), ("l", 0), ("s", 6),
-    ("l", 2), ("f", 5), ("l", 4), ("s", 8), ("f", 7), ("s", 3), ("l", 6), ("s", 5), ("l", 8), ("s", 7),
+    ("m", 0), ("m", 1), ("c", 0), ("m", 2), ("c", 1), ("c", 2), ("m", 3), ("c", 3), ("c", 4), ("m", 4),
+    ("c", 5), ("c", 6), ("m", 5), ("c", 7), ("c", 8), ("f", 0), ("f", 1), ("x", 2), ("f", 3), ("x", 4),
+    ("f", 6), ("f", 7), ("x", 5), ("s", 0), ("s", 1), ("x", 8), ("f", 2), ("s", 3), ("f", 4), ("l", 0),
+    ("s", 6), ("l", 1), ("s", 7), ("f", 5), ("f", 8), ("s", 2), ("s", 4), ("l", 3), ("l", 6), ("l", 7),
+    ("s", 5), ("s", 8),
 )
 PIECES = ((1, 1), (2, 0), (2, 1), (3, 0), (1, 0), (3, 1), (0, 0), (0, 1))
 
@@ -31,7 +32,7 @@
 
 
 def kernel(images, signs_far, kept_far, omega, out, signs, kept, pixels, weights, hada, column, total, packed, slabs,
-           load_sem, send_sem, recv_sem, slab_send, slab_recv, near, far, *buffers):
+           load_sem, small_sem, send_sem, own_sem, x_sem, first_sem, slab_send, slab_recv, near, far, *buffers):
     part, fromcore, fromx, z_first, z_second = (buffers[n * COUNT:(n + 1) * COUNT] for n in range(5))
     place, slab = lax.axis_index("pix"), lax.axis_index("img")
     width = images.shape[1]
@@ -43,15 +44,15 @@
     others = [{"img": (slab + step) % 8} for step in range(1, 8)]
 
     loads = []
-    for i, (_, size) in enumerate(CHUNKS):
-        here = pl.ds(STARTS[i], size)
-        loads.append(pltpu.make_async_copy(images.at[here], pixels.at[here], load_sem.at[i]))
-    loads.append(pltpu.make_async_copy(omega, weights, load_sem.at[COUNT]))
+    for group, (first, count) in enumerate(GROUPS):
+        here = pl.ds(STARTS[first], sum(CHUNKS[i][1] for i in range(first, first + count)))
+        loads.append(pltpu.make_async_copy(images.at[here], pixels.at[here], load_sem.at[group]))
     small = [
-        pltpu.make_async_copy(kept_far, kept, load_sem.at[COUNT + 1]),
-        pltpu.make_async_copy(signs_far, signs, load_sem.at[COUNT + 2]),
+        pltpu.make_async_copy(kept_far, kept, small_sem.at[0]),
+        pltpu.make_async_copy(signs_far, signs, small_sem.at[1]),
     ]
-    for load in small + loads:
+    last = pltpu.make_async_copy(omega, weights, small_sem.at[0])
+    for load in small + loads[:1]:
         load.start()
     barrier = pltpu.get_barrier_semaphore()
     beside = [{"img": slab // 4 * 4 + (slab + step) % 4} for step in (1, 3)] + [{"img": (slab + 4) % 8}]
@@ -68,6 +69,8 @@
 
     for load in small:
         load.wait()
+    for load in loads[1:] + [last]:
+        load.start()
     for i in range(4):
         row = kept[pl.ds(i * 128, 128)].reshape(1, 128)
         column[i * 128:(i + 1) * 128, :] = jnp.broadcast_to(row, (128, 128)).T
@@ -94,13 +97,11 @@
                     for half in range(2):
                         hada[halves[half]:halves[half] + 16, j * 128:(j + 1) * 128] = value[half * 16:half * 16 + 16]
 
-    sends = {}
-
-    def start(key, src, dst, peer):
-        at = len(sends)
-        copy = transfer(src, dst, send_sem.at[at], recv_sem.at[at], peer)
-        copy.start()
-        sends[key] = copy
+    def start(src, dst, recv, peer):
+        transfer(src, dst, send_sem, recv, peer).start()
+
+    def arrived(dst, recv):
+        transfer(dst, dst, send_sem, recv, sibling).wait_recv()
 
     def lines(i):
         return slice(0, 1) if CHUNKS[i][0] == "A" else slice(0, 2)
@@ -108,8 +109,7 @@
     def matmul(group):
         first, count = GROUPS[group]
         size = sum(CHUNKS[i][1] for i in range(first, first + count))
-        for i in range(first, first + count):
-            loads[i].wait()
+        loads[group].wait()
         value = lax.dot_general(
             hada[...], pixels[pl.ds(STARTS[first], size), :], (((1,), (1,)), ((), ())), preferred_element_type=jnp.float32
         )
@@ -119,18 +119,18 @@
         if first == 0:
             pl.semaphore_wait(barrier, len(greeted))
         for i in range(first, first + count):
-            start(("core", i), part[i].at[1], fromcore[i], sibling)
+            start(part[i].at[1], fromcore[i], own_sem.at[i], sibling)
 
     def first_round(i):
         rx = lines(i)
-        start(("up", i), part[i].at[0, rx, 0:2], z_first[i].at[0], above)
-        start(("down", i), part[i].at[0, rx, 2:4], z_first[i].at[1], below)
+        start(part[i].at[0, rx, 0:2], z_first[i].at[0], first_sem.at[i], above)
+        start(part[i].at[0, rx, 2:4], z_first[i].at[1], first_sem.at[i], below)
 
     def core_done(i):
-        sends["core", i].wait_recv()
+        arrived(fromcore[i], own_sem.at[i])
         if CHUNKS[i][0] == "A":
             part[i][0, 1] = part[i][0, 1] + fromcore[i][1]
-            start(("x", i), part[i].at[0, 1], fromx[i], across)
+            start(part[i].at[0, 1], fromx[i], x_sem.at[i], across)
             part[i][0, 0] = part[i][0, 0] + fromcore[i][0]
         else:
             part[i][0, :, 0:4] = part[i][0, :, 0:4] + fromcore[i][:, 0:4]
@@ -138,19 +138,18 @@
             part[i][0, :, 4:8] = part[i][0, :, 4:8] + fromcore[i][:, 4:8]
 
     def x_done(i):
-        sends["x", i].wait_recv()
+        arrived(fromx[i], x_sem.at[i])
         part[i][0, 0, 0:4] = part[i][0, 0, 0:4] + fromx[i][0:4]
         first_round(i)
         part[i][0, 0, 4:8] = part[i][0, 0, 4:8] + fromx[i][4:8]
 
     def first_done(i):
         rx = lines(i)
-        sends["up", i].wait_recv()
+        arrived(z_first[i], first_sem.at[i])
         part[i][0, rx, 4] = part[i][0, rx, 4] + z_first[i][0, :, 1]
-        start(("up2", i), part[i].at[0, rx, 4], z_second[i].at[0], above)
-        sends["down", i].wait_recv()
+        start(part[i].at[0, rx, 4], z_second[i].at[0], own_sem.at[i], above)
         part[i][0, rx, 5] = part[i][0, rx, 5] + z_first[i][1, :, 0]
-        start(("down2", i), part[i].at[0, rx, 5], z_second[i].at[1], below)
+        start(part[i].at[0, rx, 5], z_second[i].at[1], own_sem.at[i], below)
 
     def ring_sum(i, rx):
         upper = part[i][0, rx, 6] + z_first[i][1, rx, 1] + z_second[i][0, rx]
@@ -158,21 +157,20 @@
         return upper, lower
 
     def second_done(i):
-        sends["up2", i].wait_recv()
-        sends["down2", i].wait_recv()
+        arrived(z_second[i], own_sem.at[i])
         if CHUNKS[i][0] == "A":
             finish(i, ring_sum(i, 0))
         else:
             upper, lower = ring_sum(i, 1)
             part[i][0, 1, 6] = upper
             part[i][0, 1, 7] = lower
-            start(("late", i), part[i].at[0, 1, 6:8], fromx[i], across)
+            start(part[i].at[0, 1, 6:8], fromx[i], x_sem.at[i], across)
             upper, lower = ring_sum(i, 0)
             part[i][0, 0, 6] = upper
             part[i][0, 0, 7] = lower
 
     def late_done(i):
-        sends["late", i].wait_recv()
+        arrived(fromx[i], x_sem.at[i])
         finish(i, (part[i][0, 0, 6] + fromx[i][0], part[i][0, 0, 7] + fromx[i][1]))
 
     finished = []
@@ -184,7 +182,7 @@
         rest = (robust - high.astype(jnp.float32)).astype(jnp.bfloat16)
         both = jnp.concatenate([high, rest], axis=0)
         if not finished:
-            loads[COUNT].wait()
+            last.wait()
         term = jnp.dot(both, weights[pl.ds(STARTS[i], CHUNKS[i][1]), :], preferred_element_type=jnp.float32)
         term = term[:32] + term[32:]
         for n in range(2):
@@ -205,26 +203,21 @@
     for n in range(8):
         lanes = slice(n % 4 * 32, n % 4 * 32 + 32)
         packed[n] = jnp.concatenate([total[n // 4, 8 * q:8 * q + 8, lanes] for q in range(4)], axis=1)
-    final = []
     for step, peer in enumerate(others):
-        copy = transfer(packed.at[peer["img"]], slabs.at[step], slab_send.at[step], slab_recv.at[step], peer)
-        copy.start()
-        final.append(copy)
-    for copy in sends.values():
-        copy.wait_send()
+        transfer(packed.at[peer["img"]], slabs.at[step], slab_send, slab_recv, peer).start()
+    sent = pixels.at[pl.ds(0, 480 * 4 * pixels.shape[0] // (2 * width))]
+    transfer(sent, sent, send_sem, slab_recv, sibling).wait_send()
+    transfer(slabs, slabs, slab_send, slab_recv, sibling).wait_recv()
     result = packed[slab]
-    for step, copy in enumerate(final):
-        copy.wait_recv()
+    for step in range(len(others)):
         result = result + slabs[step]
     block = jnp.concatenate([result[:, 32 * q:32 * q + 32] for q in range(4)], axis=0)
     out[...] = block.T
-    for copy in final:
-        copy.wait_send()
+    transfer(slabs, slabs, slab_send, slab_recv, sibling).wait_send()
 
 
 def local(images, signs, kept, omega):
     rows, width = images.shape
-    copies = 6 * COUNT
     scratch = [
         pltpu.VMEM(signs.shape, jnp.int32),
         pltpu.VMEM(kept.shape, jnp.int32),
@@ -235,11 +228,14 @@
         pltpu.VMEM((2, 32, 128), jnp.float32),
         pltpu.VMEM((8, 8, 128), jnp.float32),
         pltpu.VMEM((7, 8, 128), jnp.float32),
-        pltpu.SemaphoreType.DMA((COUNT + 3,)),
-        pltpu.SemaphoreType.DMA((copies,)),
-        pltpu.SemaphoreType.DMA((copies,)),
-        pltpu.SemaphoreType.DMA((7,)),
-        pltpu.SemaphoreType.DMA((7,)),
+        pltpu.SemaphoreType.DMA((len(GROUPS),)),
+        pltpu.SemaphoreType.DMA((2,)),
+        pltpu.SemaphoreType.DMA,
+        pltpu.SemaphoreType.DMA((COUNT,)),
+        pltpu.SemaphoreType.DMA((COUNT,)),
+        pltpu.SemaphoreType.DMA((COUNT,)),
+        pltpu.SemaphoreType.DMA,
+        pltpu.SemaphoreType.DMA,
         pltpu.SemaphoreType.REGULAR,
         pltpu.SemaphoreType.REGULAR,
     ]

time: 33.1 us -> 32.7 us (0.988)
  Pallas kernels: 32.4 us -> 31.9 us
    pallas_call x1, Pallas kernels: 32.4 us -> 31.9 us  [local(): pl.pallas_call(kernel, out_shape=jax.ShapeDtypeStruct((32, 32), jnp.float...]
where the time goes in v4:
time: 32.7 us; the launch traced here: 32.6 us
  Pallas kernels  31.9 us (98%)
  local copies, waits for them, and re-layouts  0.61 us (2%)
    pallas_call x1, Pallas kernels, local(): pl.pallas_call(kernel, out_shape=jax.ShapeDtypeStruct((32, 32), jnp.float...  31.9 us

profile of v4, /device:TPU:0, one launch (start us, length us, event | category | flops | bytes accessed | tf_op | source)
XLA Modules:
  0.0 32.6 jit_solution(4186012874331928497)
XLA Ops:
  0.0 31.9 %sketch.1 = f32[32,32]{1,0:T(8,128)S(1)} custom-call(bf16[2048,1024]{1,0:T(8,128)(2,1)} %images.1, s32[1024]{0:T(1024)} %signs_far.1, s32[512]{0:T(512)} %kept_far.1, bf16[2048,256]{1,0:T(8,128)(2,1)} %omega.1), custom_call_target="tpu_custom_call" | custom-call | flops 2147483648 | bytes 5242880 | tf_op jit(solution)/shard_map/sketch/pallas_call | solution.py:248
  31.9 0.6 %copy.6 = f32[32,32]{1,0:T(8,128)} copy(f32[32,32]{1,0:T(8,128)S(1)} %sketch.1) | data formatting | bytes 8192

commit v5 on v4

--- a/solution.py
+++ b/solution.py
@@ -10,19 +10,18 @@
 NPIX = 16384
 MESH = pl.DeviceIdType.MESH
 CHUNKS = (
-    ("B", 256), ("B", 256), ("A", 256), ("B", 384), ("A", 128), ("A", 256), ("B", 128), ("B", 256), ("A", 128),
+    ("A", 128), ("B", 256), ("A", 256), ("A", 256), ("B", 256), ("B", 256), ("B", 256), ("D", 256), ("D", 128),
 )
 COUNT = len(CHUNKS)
 STARTS = [sum(size for _, size in CHUNKS[:i]) for i in range(COUNT)]
-GROUPS = ((0, 1), (1, 2), (3, 2), (5, 2), (7, 1), (8, 1))
+GROUPS = ((0, 2), (2, 2), (4, 1), (5, 2), (7, 2))
 ORDER = (
-    ("m", 0), ("m", 1), ("c", 0), ("m", 2), ("c", 1), ("c", 2), ("m", 3), ("c", 3), ("c", 4), ("m", 4),
-    ("c", 5), ("c", 6), ("m", 5), ("c", 7), ("c", 8), ("f", 0), ("f", 1), ("x", 2), ("f", 3), ("x", 4),
-    ("f", 6), ("f", 7), ("x", 5), ("s", 0), ("s", 1), ("x", 8), ("f", 2), ("s", 3), ("f", 4), ("l", 0),
-    ("s", 6), ("l", 1), ("s", 7), ("f", 5), ("f", 8), ("s", 2), ("s", 4), ("l", 3), ("l", 6), ("l", 7),
-    ("s", 5), ("s", 8),
+    ("m", 0), ("m", 1), ("c", 0), ("c", 1), ("m", 2), ("c", 2), ("c", 3), ("m", 3), ("c", 4), ("m", 4),
+    ("c", 5), ("c", 6), ("c", 7), ("c", 8), ("x", 0), ("f", 1), ("x", 2), ("f", 4), ("f", 5), ("x", 3),
+    ("f", 6), ("f", 0), ("s", 1), ("f", 2), ("x", 7), ("s", 4), ("s", 5), ("x", 8), ("f", 3), ("l", 1),
+    ("s", 6), ("s", 0), ("s", 2), ("l", 4), ("l", 5), ("s", 7), ("l", 6), ("s", 3), ("s", 8),
 )
-PIECES = ((1, 1), (2, 0), (2, 1), (3, 0), (1, 0), (3, 1), (0, 0), (0, 1))
+PIECES = ((1, 0), (1, 1), (2, 0), (2, 1), (3, 0), (3, 1), (0, 0), (0, 1))
 
 
 def transfer(src, dst, send, recv, peer):
@@ -41,6 +40,7 @@
     across = {"pix": z * 4 + (1 - x) * 2 + core}
     above = {"pix": (z + 1) % 4 * 4 + x * 2 + core}
     below = {"pix": (z + 3) % 4 * 4 + x * 2 + core}
+    opposite = {"pix": (z + 2) % 4 * 4 + x * 2 + core}
     others = [{"img": (slab + step) % 8} for step in range(1, 8)]
 
     loads = []
@@ -104,7 +104,7 @@
         transfer(dst, dst, send_sem, recv, sibling).wait_recv()
 
     def lines(i):
-        return slice(0, 1) if CHUNKS[i][0] == "A" else slice(0, 2)
+        return slice(0, 2) if CHUNKS[i][0] == "B" else slice(0, 1)
 
     def matmul(group):
         first, count = GROUPS[group]
@@ -123,31 +123,37 @@
 
     def first_round(i):
         rx = lines(i)
-        start(part[i].at[0, rx, 0:2], z_first[i].at[0], first_sem.at[i], above)
-        start(part[i].at[0, rx, 2:4], z_first[i].at[1], first_sem.at[i], below)
+        if CHUNKS[i][0] == "D":
+            start(part[i].at[0, 0, 2:4], z_first[i].at[2, 0], first_sem.at[i], opposite)
+            start(part[i].at[0, 0, 0:2], z_first[i].at[0, 0], first_sem.at[i], above)
+            start(part[i].at[0, 0, 4:6], z_first[i].at[1, 0], first_sem.at[i], below)
+        else:
+            start(part[i].at[0, rx, 1:3], z_first[i].at[0], first_sem.at[i], above)
+            start(part[i].at[0, rx, 3:5], z_first[i].at[1], first_sem.at[i], below)
 
     def core_done(i):
         arrived(fromcore[i], own_sem.at[i])
-        if CHUNKS[i][0] == "A":
+        if CHUNKS[i][0] == "B":
+            part[i][0, :, 1:5] = part[i][0, :, 1:5] + fromcore[i][:, 1:5]
+            first_round(i)
+            part[i][0, :, 0:1] = part[i][0, :, 0:1] + fromcore[i][:, 0:1]
+            part[i][0, :, 5:8] = part[i][0, :, 5:8] + fromcore[i][:, 5:8]
+        else:
             part[i][0, 1] = part[i][0, 1] + fromcore[i][1]
             start(part[i].at[0, 1], fromx[i], x_sem.at[i], across)
             part[i][0, 0] = part[i][0, 0] + fromcore[i][0]
-        else:
-            part[i][0, :, 0:4] = part[i][0, :, 0:4] + fromcore[i][:, 0:4]
-            first_round(i)
-            part[i][0, :, 4:8] = part[i][0, :, 4:8] + fromcore[i][:, 4:8]
 
     def x_done(i):
         arrived(fromx[i], x_sem.at[i])
-        part[i][0, 0, 0:4] = part[i][0, 0, 0:4] + fromx[i][0:4]
+        part[i][0, 0, 0:6] = part[i][0, 0, 0:6] + fromx[i][0:6]
         first_round(i)
-        part[i][0, 0, 4:8] = part[i][0, 0, 4:8] + fromx[i][4:8]
+        part[i][0, 0, 6:8] = part[i][0, 0, 6:8] + fromx[i][6:8]
 
     def first_done(i):
         rx = lines(i)
         arrived(z_first[i], first_sem.at[i])
-        part[i][0, rx, 4] = part[i][0, rx, 4] + z_first[i][0, :, 1]
-        start(part[i].at[0, rx, 4], z_second[i].at[0], own_sem.at[i], above)
+        part[i][0, rx, 0] = part[i][0, rx, 0] + z_first[i][0, :, 1]
+        start(part[i].at[0, rx, 0], z_second[i].at[0], own_sem.at[i], above)
         part[i][0, rx, 5] = part[i][0, rx, 5] + z_first[i][1, :, 0]
         start(part[i].at[0, rx, 5], z_second[i].at[1], own_sem.at[i], below)
 
@@ -157,6 +163,11 @@
         return upper, lower
 
     def second_done(i):
+        if CHUNKS[i][0] == "D":
+            arrived(z_first[i], first_sem.at[i])
+            both = part[i][0, 0, 6:8] + z_first[i][0, 0] + z_first[i][1, 0] + z_first[i][2, 0]
+            finish(i, (both[0], both[1]))
+            return
         arrived(z_second[i], own_sem.at[i])
         if CHUNKS[i][0] == "A":
             finish(i, ring_sum(i, 0))
@@ -239,11 +250,11 @@
         pltpu.SemaphoreType.REGULAR,
         pltpu.SemaphoreType.REGULAR,
     ]
-    lines = [1 if kind == "A" else 2 for kind, _ in CHUNKS]
+    lines = [2 if kind == "B" else 1 for kind, _ in CHUNKS]
     scratch += [pltpu.VMEM((2, 2, 8, 16, size), jnp.float32) for _, size in CHUNKS]
     scratch += [pltpu.VMEM((2, 8, 16, size), jnp.float32) for _, size in CHUNKS]
-    scratch += [pltpu.VMEM((8 if kind == "A" else 2, 16, size), jnp.float32) for kind, size in CHUNKS]
-    scratch += [pltpu.VMEM((2, n, 2, 16, size), jnp.float32) for n, (_, size) in zip(lines, CHUNKS)]
+    scratch += [pltpu.VMEM((2 if kind == "B" else 8, 16, size), jnp.float32) for kind, size in CHUNKS]
+    scratch += [pltpu.VMEM((3 if kind == "D" else 2, n, 2, 16, size), jnp.float32) for n, (kind, size) in zip(lines, CHUNKS)]
     scratch += [pltpu.VMEM((2, n, 16, size), jnp.float32) for n, (_, size) in zip(lines, CHUNKS)]
     return pl.pallas_call(
         kernel,

time: 32.7 us -> 31.7 us (0.969)
  Pallas kernels: 31.9 us -> 31 us
    pallas_call x1, Pallas kernels: 31.9 us -> 31 us  [local(): pl.pallas_call(kernel, out_shape=jax.ShapeDtypeStruct((32, 32), jnp.float...]
where the time goes in v5:
time: 31.7 us; the launch traced here: 31.6 us
  Pallas kernels  31 us (98%)
  local copies, waits for them, and re-layouts  0.61 us (2%)
    pallas_call x1, Pallas kernels, local(): pl.pallas_call(kernel, out_shape=jax.ShapeDtypeStruct((32, 32), jnp.float...  31 us

profile of v5, /device:TPU:0, one launch (start us, length us, event | category | flops | bytes accessed | tf_op | source)
XLA Modules:
  0.0 31.6 jit_solution(9392426193469185653)
XLA Ops:
  0.0 31.0 %sketch.1 = f32[32,32]{1,0:T(8,128)S(1)} custom-call(bf16[2048,1024]{1,0:T(8,128)(2,1)} %images.1, s32[1024]{0:T(1024)} %signs_far.1, s32[512]{0:T(512)} %kept_far.1, bf16[2048,256]{1,0:T(8,128)(2,1)} %omega.1), custom_call_target="tpu_custom_call" | custom-call | flops 2147483648 | bytes 5242880 | tf_op jit(solution)/shard_map/sketch/pallas_call | solution.py:259
  31.0 0.6 %copy.6 = f32[32,32]{1,0:T(8,128)} copy(f32[32,32]{1,0:T(8,128)S(1)} %sketch.1) | data formatting | bytes 8192

commit v6 on v5

--- a/solution.py
+++ b/solution.py
@@ -10,16 +10,16 @@
 NPIX = 16384
 MESH = pl.DeviceIdType.MESH
 CHUNKS = (
-    ("A", 128), ("B", 256), ("A", 256), ("A", 256), ("B", 256), ("B", 256), ("B", 256), ("D", 256), ("D", 128),
+    ("B", 256), ("A", 256), ("B", 256), ("A", 256), ("B", 256), ("B", 256), ("B", 128), ("D", 256), ("D", 128),
 )
 COUNT = len(CHUNKS)
 STARTS = [sum(size for _, size in CHUNKS[:i]) for i in range(COUNT)]
-GROUPS = ((0, 2), (2, 2), (4, 1), (5, 2), (7, 2))
+GROUPS = ((0, 2), (2, 2), (4, 2), (6, 3))
 ORDER = (
-    ("m", 0), ("m", 1), ("c", 0), ("c", 1), ("m", 2), ("c", 2), ("c", 3), ("m", 3), ("c", 4), ("m", 4),
-    ("c", 5), ("c", 6), ("c", 7), ("c", 8), ("x", 0), ("f", 1), ("x", 2), ("f", 4), ("f", 5), ("x", 3),
-    ("f", 6), ("f", 0), ("s", 1), ("f", 2), ("x", 7), ("s", 4), ("s", 5), ("x", 8), ("f", 3), ("l", 1),
-    ("s", 6), ("s", 0), ("s", 2), ("l", 4), ("l", 5), ("s", 7), ("l", 6), ("s", 3), ("s", 8),
+    ("m", 0), ("m", 1), ("c", 0), ("c", 1), ("m", 2), ("c", 2), ("c", 3), ("m", 3), ("c", 4), ("c", 5),
+    ("c", 6), ("c", 7), ("c", 8), ("f", 0), ("x", 1), ("f", 2), ("f", 4), ("x", 3), ("f", 5), ("f", 6),
+    ("s", 0), ("f", 1), ("x", 7), ("s", 2), ("s", 4), ("x", 8), ("f", 3), ("l", 0), ("s", 5), ("s", 6),
+    ("s", 1), ("l", 2), ("l", 4), ("s", 7), ("l", 5), ("s", 3), ("s", 8), ("l", 6),
 )
 PIECES = ((1, 0), (1, 1), (2, 0), (2, 1), (3, 0), (3, 1), (0, 0), (0, 1))
 
@@ -80,7 +80,7 @@
     def sign_of(bits):
         return (1 - 2 * (lax.population_count(bits) & 1)).astype(jnp.float32)
 
-    for rc in (1, 0):
+    def build(rc):
         for rx in range(2):
             for rz in range(4):
                 owner = (z + rz) % 4 * 4 + (x + rx) % 2 * 2 + (core + rc) % 2
@@ -97,6 +97,8 @@
                     for half in range(2):
                         hada[halves[half]:halves[half] + 16, j * 128:(j + 1) * 128] = value[half * 16:half * 16 + 16]
 
+    build(1)
+
     def start(src, dst, recv, peer):
         transfer(src, dst, send_sem, recv, peer).start()
 
@@ -110,16 +112,33 @@
         first, count = GROUPS[group]
         size = sum(CHUNKS[i][1] for i in range(first, first + count))
         loads[group].wait()
-        value = lax.dot_general(
-            hada[...], pixels[pl.ds(STARTS[first], size), :], (((1,), (1,)), ((), ())), preferred_element_type=jnp.float32
-        )
+
+        def multiply(rows):
+            return lax.dot_general(
+                hada[rows, :], pixels[pl.ds(STARTS[first], size), :], (((1,), (1,)), ((), ())),
+                preferred_element_type=jnp.float32,
+            )
+
+        def exchange():
+            for i in range(first, first + count):
+                start(part[i].at[1], fromcore[i], own_sem.at[i], sibling)
+
+        if first == 0:
+            for rc in (1, 0):
+                value = multiply(slice(rc * 256, rc * 256 + 256))
+                for i in range(first, first + count):
+                    at = STARTS[i] - STARTS[first]
+                    part[i][rc] = value[:, at:at + CHUNKS[i][1]].reshape(part[i].shape[1:])
+                if rc == 1:
+                    pl.semaphore_wait(barrier, len(greeted))
+                    exchange()
+                    build(0)
+            return
+        value = multiply(slice(0, 512))
         for i in range(first, first + count):
             at = STARTS[i] - STARTS[first]
             part[i][...] = value[:, at:at + CHUNKS[i][1]].reshape(part[i].shape)
-        if first == 0:
-            pl.semaphore_wait(barrier, len(greeted))
-        for i in range(first, first + count):
-            start(part[i].at[1], fromcore[i], own_sem.at[i], sibling)
+        exchange()
 
     def first_round(i):
         rx = lines(i)

time: 31.7 us -> 30.9 us (0.975)
  Pallas kernels: 31 us -> 30.1 us
    pallas_call x1, Pallas kernels: 31 us -> 30.1 us  [local(): pl.pallas_call(kernel, out_shape=jax.ShapeDtypeStruct((32, 32), jnp.float...]
where the time goes in v6:
time: 30.9 us; the launch traced here: 30.7 us
  Pallas kernels  30.1 us (97%)
  local copies, waits for them, and re-layouts  0.61 us (2%)
    pallas_call x1, Pallas kernels, local(): pl.pallas_call(kernel, out_shape=jax.ShapeDtypeStruct((32, 32), jnp.float...  30.1 us

profile of v6, /device:TPU:0, one launch (start us, length us, event | category | flops | bytes accessed | tf_op | source)
XLA Modules:
  0.0 30.7 jit_solution(12807102512009635991)
XLA Ops:
  0.0 30.1 %sketch.1 = f32[32,32]{1,0:T(8,128)S(1)} custom-call(bf16[2048,1024]{1,0:T(8,128)(2,1)} %images.1, s32[1024]{0:T(1024)} %signs_far.1, s32[512]{0:T(512)} %kept_far.1, bf16[2048,256]{1,0:T(8,128)(2,1)} %omega.1), custom_call_target="tpu_custom_call" | custom-call | flops 2147483648 | bytes 5242880 | tf_op jit(solution)/shard_map/sketch/pallas_call | solution.py:278
  30.1 0.6 %copy.6 = f32[32,32]{1,0:T(8,128)} copy(f32[32,32]{1,0:T(8,128)S(1)} %sketch.1) | data formatting | bytes 8192

commit v7 on v6

--- a/solution.py
+++ b/solution.py
@@ -41,7 +41,10 @@
     above = {"pix": (z + 1) % 4 * 4 + x * 2 + core}
     below = {"pix": (z + 3) % 4 * 4 + x * 2 + core}
     opposite = {"pix": (z + 2) % 4 * 4 + x * 2 + core}
-    others = [{"img": (slab + step) % 8} for step in range(1, 8)]
+    others = [
+        {"img": (slab // 4 + half) % 2 * 4 + (slab + step) % 4}
+        for half, step in ((1, 2), (1, 1), (1, 3), (0, 2), (1, 0), (0, 1), (0, 3))
+    ]
 
     loads = []
     for group, (first, count) in enumerate(GROUPS):

time: 30.9 us -> 30.9 us (level)
  no operation moved by 1% of the time
where the time goes in v7:
time: 30.9 us; the launch traced here: 30.8 us
  Pallas kernels  30.2 us (98%)
  local copies, waits for them, and re-layouts  0.61 us (2%)
    pallas_call x1, Pallas kernels, local(): pl.pallas_call(kernel, out_shape=jax.ShapeDtypeStruct((32, 32), jnp.float...  30.2 us

profile of v7, /device:TPU:0, one launch (start us, length us, event | category | flops | bytes accessed | tf_op | source)
XLA Modules:
  0.0 30.8 jit_solution(6485458642288527441)
XLA Ops:
  0.0 30.2 %sketch.1 = f32[32,32]{1,0:T(8,128)S(1)} custom-call(bf16[2048,1024]{1,0:T(8,128)(2,1)} %images.1, s32[1024]{0:T(1024)} %signs_far.1, s32[512]{0:T(512)} %kept_far.1, bf16[2048,256]{1,0:T(8,128)(2,1)} %omega.1), custom_call_target="tpu_custom_call" | custom-call | flops 2147483648 | bytes 5242880 | tf_op jit(solution)/shard_map/sketch/pallas_call | solution.py:281
  30.2 0.6 %copy.6 = f32[32,32]{1,0:T(8,128)} copy(f32[32,32]{1,0:T(8,128)S(1)} %sketch.1) | data formatting | bytes 8192

commit v8 on v7

--- a/solution.py
+++ b/solution.py
@@ -10,16 +10,16 @@
 NPIX = 16384
 MESH = pl.DeviceIdType.MESH
 CHUNKS = (
-    ("B", 256), ("A", 256), ("B", 256), ("A", 256), ("B", 256), ("B", 256), ("B", 128), ("D", 256), ("D", 128),
+    ("B", 256), ("A", 256), ("B", 256), ("A", 256), ("B", 256), ("D", 256), ("B", 256), ("B", 128), ("D", 128),
 )
 COUNT = len(CHUNKS)
 STARTS = [sum(size for _, size in CHUNKS[:i]) for i in range(COUNT)]
 GROUPS = ((0, 2), (2, 2), (4, 2), (6, 3))
 ORDER = (
     ("m", 0), ("m", 1), ("c", 0), ("c", 1), ("m", 2), ("c", 2), ("c", 3), ("m", 3), ("c", 4), ("c", 5),
-    ("c", 6), ("c", 7), ("c", 8), ("f", 0), ("x", 1), ("f", 2), ("f", 4), ("x", 3), ("f", 5), ("f", 6),
-    ("s", 0), ("f", 1), ("x", 7), ("s", 2), ("s", 4), ("x", 8), ("f", 3), ("l", 0), ("s", 5), ("s", 6),
-    ("s", 1), ("l", 2), ("l", 4), ("s", 7), ("l", 5), ("s", 3), ("s", 8), ("l", 6),
+    ("c", 6), ("c", 7), ("c", 8), ("f", 0), ("x", 1), ("f", 2), ("f", 4), ("x", 3), ("f", 6), ("f", 7),
+    ("s", 0), ("f", 1), ("x", 5), ("s", 2), ("s", 4), ("x", 8), ("f", 3), ("l", 0), ("s", 6), ("s", 7),
+    ("s", 1), ("l", 2), ("l", 4), ("s", 5), ("l", 6), ("s", 3), ("s", 8), ("l", 7),
 )
 PIECES = ((1, 0), (1, 1), (2, 0), (2, 1), (3, 0), (3, 1), (0, 0), (0, 1))
 

time: 30.9 us -> 30.9 us (level)
  no operation moved by 1% of the time
where the time goes in v8:
time: 30.9 us; the launch traced here: 30.8 us
  Pallas kernels  30.2 us (98%)
  local copies, waits for them, and re-layouts  0.61 us (2%)
    pallas_call x1, Pallas kernels, local(): pl.pallas_call(kernel, out_shape=jax.ShapeDtypeStruct((32, 32), jnp.float...  30.2 us

profile of v8, /device:TPU:0, one launch (start us, length us, event | category | flops | bytes accessed | tf_op | source)
XLA Modules:
  0.0 30.8 jit_solution(3096048758633624310)
XLA Ops:
  0.0 30.2 %sketch.1 = f32[32,32]{1,0:T(8,128)S(1)} custom-call(bf16[2048,1024]{1,0:T(8,128)(2,1)} %images.1, s32[1024]{0:T(1024)} %signs_far.1, s32[512]{0:T(512)} %kept_far.1, bf16[2048,256]{1,0:T(8,128)(2,1)} %omega.1), custom_call_target="tpu_custom_call" | custom-call | flops 2147483648 | bytes 5242880 | tf_op jit(solution)/shard_map/sketch/pallas_call | solution.py:281
  30.2 0.6 %copy.6 = f32[32,32]{1,0:T(8,128)} copy(f32[32,32]{1,0:T(8,128)S(1)} %sketch.1) | data formatting | bytes 8192
